TPU v7x, 128 devices: a whole 4x4x4 slice. The times are simulated.
128 devices in a mesh: axial: 8 (over y, core), azim: 16 (over z, x).
Axes of the slice: x: 4, y: 4, z: 4, core: 2. Of those that a mesh axis runs over, the one named last changes fastest.
Arguments:
- surface_pos: float32 [3, 131072], P(None, ('axial', 'azim')), may hold values from 0 to 1
- surface_coef: float32 [3, 131072], P(None, ('axial', 'azim')), may hold values from -3 to 3
- send_rows: int32 [128, 512], P(('axial', 'azim')), may hold values from 0 to 1023
- volume_pos: float32 [3, 8388608], P(None, ('axial', 'azim')), may hold values from 0 to 1
- relay_order: int32 [128, 65536], P(('axial', 'azim')), may hold values from 0 to 65535, each once within a row
- block_cols: int32 [16384, 8], P(('axial', 'azim')), may hold values from 0 to 511, as said below
- block_count: int32 [16384], P(('axial', 'azim')), may hold values from 1 to 8
Outputs:
- displacement: float32 [3, 8388608], P(None, ('axial', 'azim'))
Inputs may be any that keep to these rules, and one draw needn't show every extreme that they name: `block_cols`: A row block on axial slab a lists only center blocks owned by slabs a - 1, a, a + 1; some row block lists 8 live entries.
All inputs are finite; a program needn't handle non-finite values.
Results may differ from a plain program's by a relative error of at most 0.0003.
Values sent between devices are 32-bit elements; how exact they have to be, the bound alone decides.
No kernel may reach another device: no remote copies, remote signals or barrier semaphores. Data moves between devices by JAX's collectives and lax.ppermute only.
A program may use at most 192 MiB of HBM per device.

v0:
```python
import functools
import jax
import jax.numpy as jnp
from jax import lax
from jax.experimental import pallas as pl
from jax.experimental.pallas import tpu as pltpu
from jax.sharding import PartitionSpec as P

F32 = jnp.float32
BF16 = jnp.bfloat16
LANES = 128
CHUNK = 4096
SLOTS = 4
BATCH = 1024


def pieces(value, count):
    out = []
    for _ in range(count):
        part = value.astype(BF16).astype(F32)
        out.append(part)
        value = value - part
    return out


def build_rows(pos_ref, rows):
    held_rows = rows.shape[0]

    def build(step, carry):
        start = pl.multiple_of(step * LANES, LANES)
        x = jnp.concatenate(
            [pos_ref[:, pl.ds(g * held_rows + start, LANES)] for g in range(4)], 1
        )
        x1, x2 = pieces(x * 2.0 - 1.0, 2)
        held = x1 + x2
        n1, n2, n3 = pieces(jnp.sum(held * held, axis=0, keepdims=True), 3)
        one, zero = jnp.ones_like(n1), jnp.zeros_like(n1)
        v1 = jnp.concatenate([x1, n1, one, n3, one, zero], 0)
        v2 = jnp.concatenate([x2, n2, zero, zero, zero, zero], 0)
        stacked = jnp.concatenate(
            [v[:, g * LANES : (g + 1) * LANES] for g in range(4) for v in (v1, v1, v2, v2)], 0
        )
        rows[pl.ds(start, LANES), :] = stacked.T
        return carry

    lax.fori_loop(0, held_rows // LANES, build, 0, unroll=4)


def gather_kernel(order_ref, source_ref, pos_ref, out_ref, rows, *rest):
    taken, ids, sems = rest[:2], rest[2 : 2 + SLOTS], rest[2 + SLOTS]
    steps = pos_ref.shape[1] // CHUNK

    def fetch(step, slot):
        start = pl.multiple_of(step * CHUNK + slot * BATCH, BATCH)
        source = source_ref.at[pl.ds(start, BATCH)]
        return pltpu.make_async_copy(source, ids[slot], sems.at[slot])

    def turn(held, start):
        for part in range(BATCH // LANES):
            flat = held[part * LANES : (part + 1) * LANES, :].T
            group = order_ref[pl.ds(start // LANES + part, 1), :] >> (rows.shape[0].bit_length() - 1)
            value = flat[0:32]
            for g in range(1, 4):
                value = jnp.where(group == g, flat[32 * g : 32 * (g + 1)], value)
            at = pl.ds(pl.multiple_of(start + part * LANES, LANES), LANES)
            out_ref[:, at] = value.astype(BF16)

    for slot in range(SLOTS):
        fetch(0, slot).start()
    build_rows(pos_ref, rows)

    def one_step(step, carry):
        for slot in range(SLOTS):
            fetch(step, slot).wait()
            for k in range(BATCH):
                taken[slot % 2][pl.ds(k, 1), :] = rows[pl.ds(ids[slot][k], 1), :]
            turn(taken[1 - slot % 2], jnp.maximum(step * CHUNK + (slot - 1) * BATCH, 0))

            @pl.when(step + 1 < steps)
            def _():
                fetch(step + 1, slot).start()

        return carry

    lax.fori_loop(0, steps, one_step, 0)
    turn(taken[(SLOTS - 1) % 2], steps * CHUNK - BATCH)


def gather_rows(order, pos):
    nodes = pos.shape[1]
    vmem = pl.BlockSpec(memory_space=pltpu.VMEM)
    return pl.pallas_call(
        gather_kernel,
        in_specs=[vmem, pl.BlockSpec(memory_space=pl.ANY), vmem],
        out_specs=vmem,
        out_shape=jax.ShapeDtypeStruct((32, nodes), BF16),
        scratch_shapes=[pltpu.VMEM((nodes // 4, LANES), F32)]
        + [pltpu.VMEM((BATCH, LANES), F32) for _ in range(2)]
        + [pltpu.SMEM((BATCH,), jnp.int32) for _ in range(SLOTS)]
        + [pltpu.SemaphoreType.DMA((SLOTS,))],
        compiler_params=pltpu.CompilerParams(vmem_limit_bytes=58 * 2**20),
        cost_estimate=pl.CostEstimate(flops=10**9, bytes_accessed=100 * 2**20, transcendentals=0),
        name="gather_rows",
    )(order.reshape(-1, LANES), order & (nodes // 4 - 1), pos)


IDS = 4


def segments(width):
    return lax.broadcasted_iota(jnp.int32, (1, LANES), 1) // width


def build_table(offset, sent_ref, turned, table, cols, counts):
    owners = 48
    for row in range(12):
        turned[row] = sent_ref[:, row, :].T
    live = jnp.zeros((8, LANES), F32)
    for j in range(8):
        listed = turned[j, owners : owners + 8, :]
        cols[j * 8 : (j + 1) * 8, :] = (listed.astype(jnp.int32) - offset * 4) * 24
        live = live + jnp.where(listed >= 0.0, 1.0, 0.0)
    counts[...] = live.astype(jnp.int32)
    segment = segments(32)
    for q in range(4):
        comps = []
        for c in range(6):
            value = None
            for k in range(4):
                row = c * 4 + k
                part = turned[row % 12, 64 * (row // 12) : 64 * (row // 12) + owners, :]
                if k != q:
                    part = pltpu.roll(part, (32 * (k - q)) % LANES, 1)
                value = part if value is None else jnp.where(segment == k, part, value)
            comps.append(value)
        first, second, total = [], [], None
        for c in range(3):
            c1, c2 = pieces(comps[c] * 2.0 - 1.0, 2)
            held = c1 + c2
            total = held * held if total is None else total + held * held
            first.append(-2.0 * c1)
            second.append(-2.0 * c2)
        m1, m2, m3 = pieces(total, 3)
        one, zero = jnp.ones_like(m1), jnp.zeros_like(m1)
        high, low = [], []
        for c in range(3):
            h, l = pieces(4.0 * comps[3 + c], 2)
            high.append(h)
            low.append(l)
        rows = first + [one, m1, one, m3, zero]
        rows += second + [zero, m2, zero, zero, zero]
        rows += high + low + [zero, zero]
        for f, value in enumerate(rows):
            table[pl.ds(q * 24 + f, owners, stride=96), :] = value


def evaluate_kernel(where_ref, sent_any, order_ref, points_any, out_ref, *scratch):
    placed, turned, table, square, weights, centers, totals, results, cols, counts = scratch[:10]
    cols_smem, counts_smem, state = scratch[10:13]
    ids, sems, list_sem = scratch[13 : 13 + IDS], scratch[13 + IDS], scratch[14 + IDS]
    sent_ref, points_ref = scratch[15 + IDS :]
    blocks = points_ref.shape[1] // 512
    column = where_ref[0] * 16

    def fetch(block, slot):
        return pltpu.make_async_copy(order_ref.at[block], ids[slot], sems.at[slot])

    for slot in range(IDS):
        fetch(slot, slot).start()
    arrive = pltpu.make_async_copy(sent_any, sent_ref, list_sem.at[2])
    arrive.start()
    follow = pltpu.make_async_copy(points_any, points_ref, list_sem.at[3])
    follow.start()
    arrive.wait()
    build_table(where_ref[1], sent_ref, turned, table, cols, counts)
    waits = (
        pltpu.make_async_copy(cols, cols_smem, list_sem.at[0]),
        pltpu.make_async_copy(counts, counts_smem, list_sem.at[1]),
    )
    for wait in waits:
        wait.start()
    for wait in waits:
        wait.wait()
    follow.wait()

    def live(block):
        return counts_smem[block & 7, column + (block >> 3)]

    def chosen(block, j):
        return cols_smem[j * 8 + (block & 7), column + (block >> 3)]

    def following(block, j):
        last = j + 1 >= live(block)
        after = jnp.where(last, jnp.minimum(block + 1, blocks - 1), block)
        return after, jnp.where(last, 0, j + 1)

    def bring(row):
        held = table[pl.ds(pl.multiple_of(row, 8), 16), :]
        centers[...] = jnp.concatenate([held, held], 0).T.astype(BF16)

    def measure(block):
        nodes = points_ref[:, pl.ds(pl.multiple_of(block * 512, 512), 512)]
        return jnp.dot(centers[...], nodes, preferred_element_type=F32)

    def contract(row):
        held = table[pl.ds(pl.multiple_of(row + 16, 8), 8), :].astype(BF16)
        coefs = jnp.concatenate([held, held], 1)
        held = jnp.concatenate([weights[part] for part in range(4)], 1)
        return jnp.dot(coefs, held, preferred_element_type=F32)

    def weigh(part):
        value = square[:, part * LANES : (part + 1) * LANES]
        value = jnp.minimum(jnp.maximum(value, 1e-12), 1.0)
        dist = value * lax.rsqrt(value)
        left = 1.0 - dist
        twice = left * left
        weight = (twice * twice) * (0.25 + dist)
        high = weight.astype(BF16)
        weights[part, 0:LANES, :] = high
        weights[part, LANES:, :] = (weight - high.astype(F32)).astype(BF16)

    def turn(slot):
        for part in range(4):
            held = totals[slot % 2, :, part * LANES : (part + 1) * LANES]
            results[slot % 2, part * LANES : (part + 1) * LANES, :] = jnp.concatenate([held] * 16, 0).T

    def place(slot, parts):
        for part in parts:
            for k in range(LANES):
                row = results[slot % 2, pl.ds(part * LANES + k, 1), :]
                placed[pl.ds(ids[slot][part, k], 1), :] = row

    def advance(slot, block, j, parts, ready):
        row, coming, node_block, node_j = state[1], state[2], state[3], state[4]
        added = contract(state[0])
        before = (slot - 1) % IDS
        if isinstance(j, int) and j == 0:
            alone = live(jnp.maximum(block - 1, 0)) == 1
            totals[before % 2] = jnp.where(alone, jnp.zeros_like(added), totals[before % 2]) + added
        elif isinstance(j, int) and j == 1:
            totals[slot % 2] = added
        else:
            totals[slot % 2] += added
        upcoming = measure(node_block)
        for part in range(4):
            weigh(part)
        square[...] = upcoming
        after, later = following(node_block, node_j)
        beyond = chosen(after, later)
        bring(beyond)
        state[0], state[1], state[2], state[3], state[4] = row, coming, beyond, after, later
        place((slot + 2) % IDS, parts)
        if ready:
            turn(before)

    bring(chosen(0, 0))
    square[...] = measure(0)
    after, later = following(0, 0)
    state[0], state[1], state[2] = chosen(0, 0), chosen(0, 0), chosen(after, later)
    state[3], state[4] = after, later
    bring(chosen(after, later))

    def four_blocks(step, carry):
        for slot in range(IDS):
            block = step * IDS + slot
            count = live(block)
            fetch(0, (slot + 2) % IDS).wait()

            @pl.when(count == 1)
            def _():
                advance(slot, block, 0, (0, 1, 2, 3), True)

            @pl.when(count == 2)
            def _():
                advance(slot, block, 0, (0, 1), False)
                advance(slot, block, 1, (2, 3), True)

            @pl.when(count == 3)
            def _():
                advance(slot, block, 0, (0, 1), False)
                advance(slot, block, 1, (2,), True)
                advance(slot, block, 2, (3,), False)

            @pl.when(count >= 4)
            def _():
                advance(slot, block, 0, (0,), False)
                advance(slot, block, 1, (1,), True)
                advance(slot, block, 2, (2,), False)
                advance(slot, block, 3, (3,), False)

                def more(j, carry):
                    advance(slot, block, j, (), False)
                    return carry

                lax.fori_loop(4, count, more, 0)

            @pl.when(block + 2 < blocks)
            def _():
                fetch(block + 2, (slot + 2) % IDS).start()

        return carry

    lax.fori_loop(0, blocks // IDS, four_blocks, 0)

    count = live(blocks - 1)
    added = contract(state[0])
    final = (IDS - 1) % 2
    totals[final] = jnp.where(count == 1, jnp.zeros_like(added), totals[final]) + added
    turn(IDS - 1)
    for slot in (IDS - 2, IDS - 1):
        fetch(0, slot).wait()
        place(slot, (0, 1, 2, 3))
    segment = segments(8)

    def close(group, carry):
        start = pl.multiple_of(group * 2048, 2048)
        dense = placed[pl.ds(start, LANES), :]
        for g in range(1, 16):
            part = placed[pl.ds(start + g * LANES, LANES), :]
            dense = jnp.where(segment == g, part, dense)
        flat = dense.T
        for g in range(16):
            result = flat[8 * g : 8 * g + 3] + flat[8 * g + 3 : 8 * g + 6]
            out_ref[:, pl.ds(start + g * LANES, LANES)] = result
        return carry

    lax.fori_loop(0, out_ref.shape[1] // 2048, close, 0)


def evaluate_rows(where, sent, order, points):
    nodes = points.shape[1]
    vmem = pl.BlockSpec(memory_space=pltpu.VMEM)
    return pl.pallas_call(
        evaluate_kernel,
        in_specs=[
            pl.BlockSpec(memory_space=pltpu.SMEM),
            pl.BlockSpec(memory_space=pl.ANY),
            vmem,
            pl.BlockSpec(memory_space=pl.ANY),
        ],
        out_specs=vmem,
        out_shape=jax.ShapeDtypeStruct((3, nodes), F32),
        scratch_shapes=[
            pltpu.VMEM((nodes, LANES), F32),
            pltpu.VMEM((12, LANES, LANES), F32),
            pltpu.VMEM((192 * 24, LANES), F32),
            pltpu.VMEM((LANES, 512), F32),
            pltpu.VMEM((4, 2 * LANES, LANES), BF16),
            pltpu.VMEM((LANES, 32), BF16),
            pltpu.VMEM((2, 8, 512), F32),
            pltpu.VMEM((2, 512, LANES), F32),
            pltpu.VMEM((64, LANES), jnp.int32),
            pltpu.VMEM((8, LANES), jnp.int32),
            pltpu.SMEM((64, LANES), jnp.int32),
            pltpu.SMEM((8, LANES), jnp.int32),
            pltpu.SMEM((8,), jnp.int32),
        ]
        + [pltpu.SMEM((4, LANES), jnp.int32) for _ in range(IDS)]
        + [pltpu.SemaphoreType.DMA((IDS,)), pltpu.SemaphoreType.DMA((4,))]
        + [pltpu.VMEM(sent.shape, F32), pltpu.VMEM(points.shape, BF16)],
        compiler_params=pltpu.CompilerParams(vmem_limit_bytes=58 * 2**20),
        cost_estimate=pl.CostEstimate(flops=10**10, bytes_accessed=100 * 2**20, transcendentals=0),
        name="evaluate_rows",
    )(where, sent, order.reshape(-1, 4, LANES), points)


def pick(source, index):
    return jnp.take_along_axis(source, index, axis=1, mode="promise_in_bounds")


def pack_kernel(pos_ref, coef_ref, send_ref, cols_ref, count_ref, out_ref):
    slabs, sectors = 8, 16
    lane = lax.broadcasted_iota(jnp.int32, (1, LANES), 1)
    order = lax.broadcasted_iota(jnp.int32, (8, LANES), 0)
    surface = jnp.concatenate([pos_ref[...], coef_ref[...], coef_ref[0:2]], 0)
    wanted = 4 * lax.broadcasted_iota(jnp.int32, (8, LANES), 1) + (order & 3)
    sent = None
    for part in range(4):
        held = jnp.broadcast_to(send_ref[:, part * LANES : (part + 1) * LANES], (8, LANES))
        found = pick(held, wanted & (LANES - 1))
        sent = found if sent is None else jnp.where(wanted >> 7 == part, found, sent)
    picked = []
    for k in range(4):
        node = jnp.broadcast_to(sent[k : k + 1], (8, LANES))
        value = None
        for part in range(8):
            found = pick(surface[:, part * LANES : (part + 1) * LANES], node & (LANES - 1))
            value = found if value is None else jnp.where(node >> 7 == part, found, value)
        picked.append(value)
    low = jnp.concatenate([picked[k][c : c + 1] for c in range(3) for k in range(4)], 0)
    high = jnp.concatenate([picked[k][c : c + 1] for c in range(3, 6) for k in range(4)], 0)
    listed = jnp.where(order < count_ref[...], cols_ref[...], -1).astype(F32)
    lists = [pltpu.roll(listed, (48 - 8 * z) % LANES, 1) for z in range(sectors)]
    for a in range(slabs):
        base = min(max((a - 1) * sectors, 0), (slabs - 3) * sectors)
        left = low if base == 0 else pltpu.roll(low, LANES - base, 1)
        right = pltpu.roll(high, (64 - base) % LANES, 1)
        rows = jnp.where(lane < 64, left, right)
        for z in range(sectors):
            out_ref[a * sectors + z, 0:8, :] = jnp.where(lane // 8 == 6, lists[z], rows[0:8])
            out_ref[a * sectors + z, 8:12, :] = rows[8:12]
            out_ref[a * sectors + z, 12:16, :] = rows[8:12]


def pack(*operands):
    vmem = pl.BlockSpec(memory_space=pltpu.VMEM)
    return pl.pallas_call(
        pack_kernel,
        in_specs=[vmem] * 5,
        out_specs=vmem,
        out_shape=jax.ShapeDtypeStruct((LANES, 16, LANES), F32),
        name="pack",
    )(*operands)


def per_device(
    surface_pos, surface_coef, send_rows, volume_pos, relay_order, block_cols, block_count
):
    axial = lax.axis_index("axial")
    slabs, sectors = lax.axis_size("axial"), lax.axis_size("azim")
    payload = pack(surface_pos, surface_coef, send_rows, block_cols.T, block_count[None])
    sent = lax.all_to_all(payload, ("axial", "azim"), split_axis=0, concat_axis=0, tiled=True)
    order = relay_order[0]
    points = gather_rows(order, volume_pos)
    low = jnp.clip((axial - 1) * sectors, 0, (slabs - 3) * sectors)
    where = jnp.stack([axial, low]).astype(jnp.int32)
    return evaluate_rows(where, sent, order, points)


def solution(mesh):
    placed = (
        P(None, ("axial", "azim")),
        P(None, ("axial", "azim")),
        P(("axial", "azim"), None),
        P(None, ("axial", "azim")),
        P(("axial", "azim"), None),
        P(("axial", "azim"), None),
        P(("axial", "azim")),
    )
    return jax.shard_map(
        per_device,
        mesh=mesh,
        in_specs=placed,
        out_specs=P(None, ("axial", "azim")),
        check_vma=False,
    )
```

profile of v0, /device:TPU:112, one launch (start us, length us, event | category | flops | bytes accessed | tf_op | source)
XLA Modules:
  0.0 180.5 jit_solution(13096204875919536185)
XLA Ops:
  0.0 2.1 %pack.1 = f32[128,16,128]{2,1,0:T(8,128)} custom-call(f32[3,1024]{1,0:T(4,128)} %pos_ref.2, f32[3,1024]{1,0:T(4,128)} %coef_ref.1, s32[1,512]{1,0:T(1,128)} %send_ref.1, s32[8,128]{1,0:T(8,128)} %bitcast.10, s32[1,128]{1,0:T(1,128)} %bitcast.11), custom_call_target="tpu_custom_call" | custom-call | tf_op jit(solution)/shard_map/pack/pallas_call | solution.py:407
  2.1 9.8 %all-to-all-start = ((f32[128,16,128]{2,1,0:T(8,128)}), f32[128,16,128]{2,1,0:T(8,128)S(1)}, u32[]{:S(2)}, u32[]{:S(2)}) async-start(f32[128,16,128]{2,1,0:T(8,128)} %pack.1), calls=%async_computation | async-start | bytes 2097152 | tf_op jit(solution)/shard_map/all_to_all | solution.py:422
  11.9 1.9 %broadcast_and_fusion = s32[1,65536]{1,0:T(1,128)} fusion(s32[1,65536]{1,0:T(1,128)} %param.11), kind=kLoop, calls=%fused_computation | loop fusion | flops 65536 | bytes 524288 | tf_op jit(solution)/shard_map/and | solution.py:104
  13.7 48.6 %gather_rows.1.points_any = bf16[32,65536]{1,0:T(8,128)(2,1)} custom-call(s32[512,128]{1,0:T(8,128)} %bitcast.7, s32[65536]{0:T(1024)} %bitcast.9, f32[3,65536]{1,0:T(4,128)} %pos_ref.3), custom_call_target="tpu_custom_call" | custom-call | flops 1000000000 | bytes 104857600 | tf_op jit(solution)/shard_map/gather_rows/pallas_call | solution.py:92
  62.4 0.6 pad_add_fusion.where_ref
  62.9 0.0 all-to-all-done.sent_any
  63.0 0.0 copy-start
  63.0 1.0 copy-done
  63.9 116.4 %evaluate_rows.1 = f32[3,65536]{1,0:T(4,128)} custom-call(s32[2]{0:T(128)} %pad_add_fusion.where_ref, f32[128,16,128]{2,1,0:T(8,128)} %copy-done, s32[128,4,128]{2,1,0:T(4,128)} %bitcast.8, bf16[32,65536]{1,0:T(8,128)(2,1)} %gather_rows.1.points_any), custom_call_target="tpu_custom_call" | custom-call | flops 10000000000 | bytes 104857600 | tf_op jit(solution)/shard_map/evaluate_rows/pallas_call | solution.py:333
Async XLA Ops:
  2.1 60.8 %all-to-all-start = ((f32[128,16,128]{2,1,0:T(8,128)}), f32[128,16,128]{2,1,0:T(8,128)S(1)}, u32[]{:S(2)}, u32[]{:S(2)}) async-start(f32[128,16,128]{2,1,0:T(8,128)} %pack.1), calls=%async_computation | async-start | bytes 2097152 | tf_op jit(solution)/shard_map/all_to_all | solution.py:422
  63.0 1.0 copy-start
where the time goes:
time: 178 us; the launch traced here: 181 us
  Pallas kernels  167 us (94%)
  starting transfers between devices  9.76 us (5%)
  other arithmetic  2.45 us (1%)
    pallas_call x1, Pallas kernels, evaluate_rows(): pl.pallas_call(evaluate_kernel, in_specs=[pl.BlockSpec(memory_space=pltpu...  116 us
    pallas_call x1, Pallas kernels, gather_rows(): pl.pallas_call(gather_kernel, in_specs=[vmem, pl.BlockSpec(memory_space=p...  48.6 us
    all_to_all x1, starting transfers between devices, per_device(): lax.all_to_all(payload, ('axial', 'azim'), split_axis=0, concat_axis=0, t...  9.76 us
  transfers between devices with their start and end apart: 1, of which 0 were waited for; matrix products, arithmetic and copies ran while one was open for 1% of the time, Pallas kernels for 27%

commit v1 on v0

--- a/solution.py
+++ b/solution.py
@@ -46,13 +46,13 @@
     lax.fori_loop(0, held_rows // LANES, build, 0, unroll=4)
 
 
-def gather_kernel(order_ref, source_ref, pos_ref, out_ref, rows, *rest):
+def gather_kernel(order_ref, pos_ref, out_ref, rows, source_ref, *rest):
     taken, ids, sems = rest[:2], rest[2 : 2 + SLOTS], rest[2 + SLOTS]
     steps = pos_ref.shape[1] // CHUNK
 
     def fetch(step, slot):
-        start = pl.multiple_of(step * CHUNK + slot * BATCH, BATCH)
-        source = source_ref.at[pl.ds(start, BATCH)]
+        start = pl.multiple_of((step * CHUNK + slot * BATCH) // LANES, BATCH // LANES)
+        source = source_ref.at[pl.ds(start, BATCH // LANES)]
         return pltpu.make_async_copy(source, ids[slot], sems.at[slot])
 
     def turn(held, start):
@@ -65,6 +65,7 @@
             at = pl.ds(pl.multiple_of(start + part * LANES, LANES), LANES)
             out_ref[:, at] = value.astype(BF16)
 
+    source_ref[...] = order_ref[...] & (rows.shape[0] - 1)
     for slot in range(SLOTS):
         fetch(0, slot).start()
     build_rows(pos_ref, rows)
@@ -73,7 +74,7 @@
         for slot in range(SLOTS):
             fetch(step, slot).wait()
             for k in range(BATCH):
-                taken[slot % 2][pl.ds(k, 1), :] = rows[pl.ds(ids[slot][k], 1), :]
+                taken[slot % 2][pl.ds(k, 1), :] = rows[pl.ds(ids[slot][k // LANES, k % LANES], 1), :]
             turn(taken[1 - slot % 2], jnp.maximum(step * CHUNK + (slot - 1) * BATCH, 0))
 
             @pl.when(step + 1 < steps)
@@ -91,17 +92,17 @@
     vmem = pl.BlockSpec(memory_space=pltpu.VMEM)
     return pl.pallas_call(
         gather_kernel,
-        in_specs=[vmem, pl.BlockSpec(memory_space=pl.ANY), vmem],
+        in_specs=[vmem, vmem],
         out_specs=vmem,
         out_shape=jax.ShapeDtypeStruct((32, nodes), BF16),
-        scratch_shapes=[pltpu.VMEM((nodes // 4, LANES), F32)]
+        scratch_shapes=[pltpu.VMEM((nodes // 4, LANES), F32), pltpu.VMEM((nodes // LANES, LANES), jnp.int32)]
         + [pltpu.VMEM((BATCH, LANES), F32) for _ in range(2)]
-        + [pltpu.SMEM((BATCH,), jnp.int32) for _ in range(SLOTS)]
+        + [pltpu.SMEM((BATCH // LANES, LANES), jnp.int32) for _ in range(SLOTS)]
         + [pltpu.SemaphoreType.DMA((SLOTS,))],
         compiler_params=pltpu.CompilerParams(vmem_limit_bytes=58 * 2**20),
         cost_estimate=pl.CostEstimate(flops=10**9, bytes_accessed=100 * 2**20, transcendentals=0),
         name="gather_rows",
-    )(order.reshape(-1, LANES), order & (nodes // 4 - 1), pos)
+    )(order.reshape(-1, LANES), pos)
 
 
 IDS = 4
@@ -154,13 +155,15 @@
             table[pl.ds(q * 24 + f, owners, stride=96), :] = value
 
 
-def evaluate_kernel(where_ref, sent_any, order_ref, points_any, out_ref, *scratch):
+def evaluate_kernel(sent_any, order_ref, points_any, out_ref, *scratch):
     placed, turned, table, square, weights, centers, totals, results, cols, counts = scratch[:10]
     cols_smem, counts_smem, state = scratch[10:13]
     ids, sems, list_sem = scratch[13 : 13 + IDS], scratch[13 + IDS], scratch[14 + IDS]
     sent_ref, points_ref = scratch[15 + IDS :]
     blocks = points_ref.shape[1] // 512
-    column = where_ref[0] * 16
+    axial = lax.axis_index("axial")
+    column = axial * 16
+    low = jnp.clip((axial - 1) * 16, 0, (lax.axis_size("axial") - 3) * 16)
 
     def fetch(block, slot):
         return pltpu.make_async_copy(order_ref.at[block], ids[slot], sems.at[slot])
@@ -172,7 +175,7 @@
     follow = pltpu.make_async_copy(points_any, points_ref, list_sem.at[3])
     follow.start()
     arrive.wait()
-    build_table(where_ref[1], sent_ref, turned, table, cols, counts)
+    build_table(low, sent_ref, turned, table, cols, counts)
     waits = (
         pltpu.make_async_copy(cols, cols_smem, list_sem.at[0]),
         pltpu.make_async_copy(counts, counts_smem, list_sem.at[1]),
@@ -327,13 +330,12 @@
     lax.fori_loop(0, out_ref.shape[1] // 2048, close, 0)
 
 
-def evaluate_rows(where, sent, order, points):
+def evaluate_rows(sent, order, points):
     nodes = points.shape[1]
     vmem = pl.BlockSpec(memory_space=pltpu.VMEM)
     return pl.pallas_call(
         evaluate_kernel,
         in_specs=[
-            pl.BlockSpec(memory_space=pltpu.SMEM),
             pl.BlockSpec(memory_space=pl.ANY),
             vmem,
             pl.BlockSpec(memory_space=pl.ANY),
@@ -361,7 +363,7 @@
         compiler_params=pltpu.CompilerParams(vmem_limit_bytes=58 * 2**20),
         cost_estimate=pl.CostEstimate(flops=10**10, bytes_accessed=100 * 2**20, transcendentals=0),
         name="evaluate_rows",
-    )(where, sent, order.reshape(-1, 4, LANES), points)
+    )(sent, order.reshape(-1, 4, LANES), points)
 
 
 def pick(source, index):
@@ -416,15 +418,11 @@
 def per_device(
     surface_pos, surface_coef, send_rows, volume_pos, relay_order, block_cols, block_count
 ):
-    axial = lax.axis_index("axial")
-    slabs, sectors = lax.axis_size("axial"), lax.axis_size("azim")
     payload = pack(surface_pos, surface_coef, send_rows, block_cols.T, block_count[None])
     sent = lax.all_to_all(payload, ("axial", "azim"), split_axis=0, concat_axis=0, tiled=True)
     order = relay_order[0]
     points = gather_rows(order, volume_pos)
-    low = jnp.clip((axial - 1) * sectors, 0, (slabs - 3) * sectors)
-    where = jnp.stack([axial, low]).astype(jnp.int32)
-    return evaluate_rows(where, sent, order, points)
+    return evaluate_rows(sent, order, points)
 
 
 def solution(mesh):

time: 178 us -> 174 us (0.978)
  the two profiles are of different devices: /device:TPU:112 before, /device:TPU:56 now
where the time goes in v1:
time: 174 us
  Pallas kernels  163 us (94%)
  starting transfers between devices  10.1 us (6%)
    pallas_call x1, Pallas kernels, evaluate_rows(): pl.pallas_call(evaluate_kernel, in_specs=[pl.BlockSpec(memory_space=pl.AN...  112 us
    pallas_call x1, Pallas kernels, gather_rows(): pl.pallas_call(gather_kernel, in_specs=[vmem, vmem], out_specs=vmem, out_...  48.7 us
    all_to_all x1, starting transfers between devices, per_device(): lax.all_to_all(payload, ('axial', 'azim'), split_axis=0, concat_axis=0, t...  10.1 us
  transfers between devices with their start and end apart: 1, of which 0 were waited for; matrix products, arithmetic and copies ran while one was open for 0% of the time, Pallas kernels for 28%

profile of v1, /device:TPU:56, one launch (start us, length us, event | category | flops | bytes accessed | tf_op | source)
XLA Modules:
  0.0 174.3 jit_solution(13937714294364682530)
XLA Ops:
  0.0 2.1 %pack.1 = f32[128,16,128]{2,1,0:T(8,128)} custom-call(f32[3,1024]{1,0:T(4,128)} %pos_ref.2, f32[3,1024]{1,0:T(4,128)} %coef_ref.1, s32[1,512]{1,0:T(1,128)} %send_ref.1, s32[8,128]{1,0:T(8,128)} %bitcast.6, s32[1,128]{1,0:T(1,128)} %bitcast.7), custom_call_target="tpu_custom_call" | custom-call | tf_op jit(solution)/shard_map/pack/pallas_call | solution.py:409
  2.1 10.1 %all-to-all-start = ((f32[128,16,128]{2,1,0:T(8,128)}), f32[128,16,128]{2,1,0:T(8,128)S(1)}, u32[]{:S(2)}, u32[]{:S(2)}) async-start(f32[128,16,128]{2,1,0:T(8,128)} %pack.1), calls=%async_computation | async-start | bytes 2097152 | tf_op jit(solution)/shard_map/all_to_all | solution.py:422
  12.2 48.7 %gather_rows.1.points_any = bf16[32,65536]{1,0:T(8,128)(2,1)} custom-call(s32[512,128]{1,0:T(8,128)} %bitcast.4, f32[3,65536]{1,0:T(4,128)} %pos_ref.3), custom_call_target="tpu_custom_call" | custom-call | flops 1000000000 | bytes 104857600 | tf_op jit(solution)/shard_map/gather_rows/pallas_call | solution.py:93
  60.9 0.0 all-to-all-done.sent_any
  60.9 0.0 copy-start
  61.0 1.0 copy-done
  61.9 112.2 %evaluate_rows.1 = f32[3,65536]{1,0:T(4,128)} custom-call(f32[128,16,128]{2,1,0:T(8,128)} %copy-done, s32[128,4,128]{2,1,0:T(4,128)} %bitcast.5, bf16[32,65536]{1,0:T(8,128)(2,1)} %gather_rows.1.points_any), custom_call_target="tpu_custom_call" | custom-call | flops 10000000000 | bytes 104857600 | tf_op jit(solution)/shard_map/evaluate_rows/pallas_call | solution.py:336
Async XLA Ops:
  2.1 58.8 %all-to-all-start = ((f32[128,16,128]{2,1,0:T(8,128)}), f32[128,16,128]{2,1,0:T(8,128)S(1)}, u32[]{:S(2)}, u32[]{:S(2)}) async-start(f32[128,16,128]{2,1,0:T(8,128)} %pack.1), calls=%async_computation | async-start | bytes 2097152 | tf_op jit(solution)/shard_map/all_to_all | solution.py:422
  60.9 1.0 copy-start
